TPU v7x, 256 devices: a whole 4x4x8 slice. The times are simulated.
256 devices in a mesh: ctx: 32 (over z, x_lo, core), head: 8 (over x_hi, y).
Axes of the slice: x: 4 (x_hi: 2, x_lo: 2; x = x_hi * 2 + x_lo), y: 4, z: 8, core: 2. Of those that a mesh axis runs over, the one named last changes fastest.
Arguments:
- kv_latent: bfloat16 [16384, 576], P('ctx'), may hold values from -4 to 4
- queries: bfloat16 [16384, 3072], P('ctx', 'head'), may hold values from -22 to 22
- grad_out: bfloat16 [16384, 2048], P('ctx', 'head'), may hold values from -6 to 6
- kv_up_weight: bfloat16 [512, 4096], P(None, 'head'), may hold values from -0.25 to 0.25
- doc_ids: int32 [16384], replicated, may hold values from 0 to 15, never falling along the last dimension, each value on 1 to 1536 neighbouring positions
Outputs:
- grad_queries: bfloat16 [16384, 3072], P('ctx', 'head')
- grad_latent: bfloat16 [16384, 576], P('ctx')
- grad_weight: float32 [512, 4096], P('ctx', 'head')
Inputs may be any that keep to these rules, and one draw needn't show every extreme that they name: `doc_ids`: document ids never fall along the sequence; every document has 1 to 1536 tokens, and one has exactly 1536.
All inputs are finite; a program needn't handle non-finite values.
Results may differ from a plain program's by a relative error of at most 0.0076.
Values may be sent and summed in bfloat16 or wider, within the bound.
A program may use at most 64 MiB of HBM per device.

v0:
```python
import math
import jax
import jax.numpy as jnp
from jax import lax
from jax.sharding import PartitionSpec as P

NOPE = 128
ROPE = 64
VDIM = 128
LATENT = 512
REACH = 3
KEY_BLOCK = 512
masked_score = -1e30


def from_behind(value, axis, steps):
    count = lax.axis_size(axis)
    initial, last = (max(0, -steps), min(count, count - steps))
    return lax.ppermute(value, axis, [(source, source + steps) for source in range(initial, last)])


def local(kv_latent, queries, grad_out, kv_up_weight, doc_ids):
    row_count = kv_latent.shape[0]
    token_total = doc_ids.shape[0]
    head_count = kv_up_weight.shape[1] // (NOPE + VDIM)
    kv_width = head_count * (NOPE + VDIM)
    score_scale = 1.0 / math.sqrt(NOPE + ROPE)
    first_row = lax.axis_index("ctx") * row_count
    window_rows = (REACH + 1) * row_count
    window_start = first_row - REACH * row_count
    earlier = [kv_latent] + [
        from_behind(kv_latent, "ctx", offset) for offset in range(1, REACH + 1)
    ]
    stacked = jnp.concatenate(earlier[::-1], axis=0)
    lifted = jnp.dot(stacked[:, :LATENT], kv_up_weight, preferred_element_type=jnp.float32)
    key_side = jnp.concatenate([lifted.astype(jnp.bfloat16), stacked[:, LATENT:]], axis=1)
    query_heads = queries.reshape(row_count, head_count, NOPE + ROPE)
    query_nope = query_heads[:, :, :NOPE]
    query_rope = query_heads[:, :, NOPE:]
    out_heads = grad_out.reshape(row_count, head_count, VDIM)
    my_docs = lax.dynamic_slice_in_dim(doc_ids, first_row, row_count)
    query_pos = first_row + jnp.arange(row_count, dtype=jnp.int32)

    def block_parts(block_index):
        block_start = (block_index * KEY_BLOCK).astype(jnp.int32)
        key_rows = lax.dynamic_slice_in_dim(key_side, block_start, KEY_BLOCK, 0)
        pairs = key_rows[:, :kv_width].reshape(KEY_BLOCK, head_count, NOPE + VDIM)
        key_nope = pairs[:, :, :NOPE]
        values = pairs[:, :, NOPE:]
        key_rope = key_rows[:, kv_width:]
        key_pos = window_start + block_start + jnp.arange(KEY_BLOCK, dtype=jnp.int32)
        key_docs = jnp.take(doc_ids, jnp.clip(key_pos, 0, token_total - 1))
        visible = (
            (my_docs[:, None] == key_docs[None, :])
            & (key_pos[None, :] <= query_pos[:, None])
            & (key_pos[None, :] >= 0)
        )
        scores = score_scale * (
            jnp.einsum("thd,khd->htk", query_nope, key_nope, preferred_element_type=jnp.float32)
            + jnp.einsum("thd,kd->htk", query_rope, key_rope, preferred_element_type=jnp.float32)
        )
        scores = jnp.where(visible[None], scores, masked_score)
        grad_probs = jnp.einsum(
            "thd,khd->htk", out_heads, values, preferred_element_type=jnp.float32
        )
        return (key_nope, values, key_rope, visible, scores, grad_probs)

    block_total = window_rows // KEY_BLOCK
    block_first = 0

    def first_pass(block_index, carry):
        row_top, row_mass, row_cross = carry
        parts = block_parts(block_index)
        visible, scores, grad_probs = (parts[3], parts[4], parts[5])
        new_top = jnp.maximum(row_top, jnp.max(scores, axis=2))
        factor = jnp.exp(row_top - new_top)
        weights = jnp.where(visible[None], jnp.exp(scores - new_top[:, :, None]), 0.0)
        return (
            new_top,
            row_mass * factor + jnp.sum(weights, axis=2),
            row_cross * factor + jnp.sum(weights * grad_probs, axis=2),
        )

    stat_shape = (head_count, row_count)
    row_top, row_mass, row_cross = lax.fori_loop(
        block_first,
        block_total,
        first_pass,
        (
            jnp.full(stat_shape, masked_score, jnp.float32),
            jnp.zeros(stat_shape, jnp.float32),
            jnp.zeros(stat_shape, jnp.float32),
        ),
    )
    log_total = row_top + jnp.log(row_mass)
    delta = row_cross / row_mass

    def second_pass(block_index, carry):
        grad_qnope, grad_qrope, key_grads = carry
        key_nope, values, key_rope, visible, scores, grad_probs = block_parts(block_index)
        weights = jnp.where(visible[None], jnp.exp(scores - log_total[:, :, None]), 0.0)
        grad_scores = (weights * (grad_probs - delta[:, :, None])).astype(jnp.bfloat16)
        weights_low = weights.astype(jnp.bfloat16)
        grad_qnope = grad_qnope + score_scale * jnp.einsum(
            "htk,khd->thd", grad_scores, key_nope, preferred_element_type=jnp.float32
        )
        grad_qrope = grad_qrope + score_scale * jnp.einsum(
            "htk,kd->thd", grad_scores, key_rope, preferred_element_type=jnp.float32
        )
        grad_keys = score_scale * jnp.einsum(
            "htk,thd->khd", grad_scores, query_nope, preferred_element_type=jnp.float32
        )
        grad_rope = score_scale * jnp.einsum(
            "htk,thd->kd", grad_scores, query_rope, preferred_element_type=jnp.float32
        )
        grad_values = jnp.einsum(
            "htk,thd->khd", weights_low, out_heads, preferred_element_type=jnp.float32
        )
        block_grad = jnp.concatenate(
            [
                jnp.concatenate([grad_keys, grad_values], axis=2).reshape(KEY_BLOCK, kv_width),
                grad_rope,
            ],
            axis=1,
        )
        key_grads = lax.dynamic_update_slice_in_dim(
            key_grads, block_grad, (block_index * KEY_BLOCK).astype(jnp.int32), 0
        )
        return (grad_qnope, grad_qrope, key_grads)

    grad_qnope, grad_qrope, key_grads = lax.fori_loop(
        block_first,
        block_total,
        second_pass,
        (
            jnp.zeros((row_count, head_count, NOPE), jnp.float32),
            jnp.zeros((row_count, head_count, ROPE), jnp.float32),
            jnp.zeros((window_rows, kv_width + ROPE), jnp.float32),
        ),
    )

    def owner_part(offset):
        return key_grads[(REACH - offset) * row_count : (REACH - offset + 1) * row_count]

    summed = owner_part(0)
    for offset in range(1, REACH + 1):
        summed = summed + from_behind(owner_part(offset), "ctx", -offset)
    kv_grad = summed[:, :kv_width].astype(jnp.bfloat16)
    rope_grad = summed[:, kv_width:]
    latent_part = lax.dot_general(
        kv_grad, kv_up_weight, (((1,), (1,)), ((), ())), preferred_element_type=jnp.float32
    )
    latent_total = lax.psum(jnp.concatenate([latent_part, rope_grad], axis=1), "head")
    latent_cols = lax.slice_in_dim(
        kv_latent, 0, lax.axis_size("ctx") * (LATENT // lax.axis_size("ctx")), axis=1
    )
    grad_weight = lax.psum_scatter(
        lax.dot_general(
            latent_cols, kv_grad, (((0,), (0,)), ((), ())), preferred_element_type=jnp.float32
        ),
        "ctx",
        scatter_dimension=0,
        tiled=True,
    )
    grad_queries = (
        jnp.concatenate([grad_qnope, grad_qrope], axis=2)
        .reshape(row_count, head_count * (NOPE + ROPE))
        .astype(jnp.bfloat16)
    )
    return (grad_queries, latent_total.astype(jnp.bfloat16), grad_weight)


def solution(mesh):
    return jax.shard_map(
        local,
        mesh=mesh,
        in_specs=(P("ctx", None), P("ctx", "head"), P("ctx", "head"), P(None, "head"), P()),
        out_specs=(P("ctx", "head"), P("ctx", None), P("ctx", "head")),
        check_vma=False,
    )
```

profile of v0, /device:TPU:24, one launch (start us, length us, event | category | flops | bytes accessed | tf_op | source)
XLA Modules:
  0.0 333.0 jit_solution(5811115365233028075)
XLA Ops:
  7.2 3.8 %collective-permute-start = (bf16[512,576]{0,1:T(8,128)(2,1)}, bf16[512,576]{0,1:T(8,128)(2,1)}, u32[]{:S(2)}, u32[]{:S(2)}) collective-permute-start(bf16[512,576]{0,1:T(8,128)(2,1)} %param.11), channel_id=1, source_target_pairs={{0,24},{8,32},{16,40},{24,48},{32,56},{40,64},{48,72},{56,80},{64,... | collective-permute-start | bytes 1769480 | tf_op jit(solution)/shard_map/ppermute | solution.py:19
  11.0 4.6 %collective-permute-start.1 = (bf16[512,576]{0,1:T(8,128)(2,1)}, bf16[512,576]{0,1:T(8,128)(2,1)}, u32[]{:S(2)}, u32[]{:S(2)}) collective-permute-start(bf16[512,576]{0,1:T(8,128)(2,1)} %param.11), channel_id=1, source_target_pairs={{0,16},{8,24},{16,32},{24,40},{32,48},{40,56},{48,64},{56,72},{64,... | collective-permute-start | bytes 1769480 | tf_op jit(solution)/shard_map/ppermute | solution.py:19
  15.6 1.6 collective-permute-start.2
  21.8 11.4 %collective-permute-done.1 = bf16[512,576]{0,1:T(8,128)(2,1)} collective-permute-done((bf16[512,576]{0,1:T(8,128)(2,1)}, bf16[512,576]{0,1:T(8,128)(2,1)}, u32[]{:S(2)}, u32[]{:S(2)}) %collective-permute-start.1) | collective-permute-done | bytes 589856 | tf_op jit(solution)/shard_map/ppermute | solution.py:19
  36.0 1.7 pad_maximum_fusion.1
  37.7 32.1 %while.36 = (s32[]{:T(128)}, f32[2,512]{1,0:T(2,128)S(1)}, f32[2,512]{1,0:T(2,128)S(1)}, f32[2,512]{1,0:T(2,128)S(1)}, s32[512]{0:T(512)S(1)}, /*index=5*/s32[]{...) while((s32[]{:T(128)}, f32[2,512]{1,0:T(2,128)S(1)}, ...), condition=%wide.region_4.6_spmd.clone, body=%wide.region_0.5_spmd.clone.sunk | while | flops 342376960 | bytes 13933842 | solution.py:85
  37.8 3.1 gather_fusion
  42.8 1.6 fusion.95
  45.8 3.1 gather_fusion
  50.8 1.6 fusion.95
  53.8 3.1 gather_fusion
  58.9 1.6 fusion.95
  61.8 3.1 gather_fusion
  66.9 1.6 fusion.95
  69.8 2.7 broadcast_in_dim.131
  72.5 46.1 %while.37 = (s32[]{:T(128)}, f32[512,2,128]{0,2,1:T(8,128)S(1)}, f32[512,2,64]{0,2,1:T(8,128)S(1)}, f32[2048,576]{0,1:T(8,128)}, bf16[2048,576]{0,1:T(8,128)(2,1...) while((s32[]{:T(128)}, f32[512,2,128]{0,2,1:T(8,128)S(1)}, ...), condition=%wide.region_6.8_spmd.clone, body=%wide.region_5.7_spmd.clone.sunk | while | flops 879502848 | bytes 26778924 | solution.py:131
  72.6 3.1 gather_fusion.1
  77.6 1.8 fusion.116
  84.1 3.1 gather_fusion.1
  89.1 1.8 fusion.116
  95.7 3.1 gather_fusion.1
  100.7 1.7 fusion.116
  107.2 3.1 gather_fusion.1
  112.2 1.7 fusion.116
  118.6 2.3 fusion.37
  125.0 2.8 collective-permute-done.3
  127.8 34.0 %collective-permute-done.5 = f32[512,576]{0,1:T(8,128)S(1)} collective-permute-done((f32[512,576]{0,1:T(8,128)S(1)}, f32[512,576]{0,1:T(8,128)S(1)}, u32[]{:S(2)}, u32[]{:S(2)}) %collective-permute-start.5) | collective-permute-done | bytes 1179680 | tf_op jit(solution)/shard_map/ppermute | solution.py:19
  161.8 12.1 %collective-permute-done.4 = f32[512,576]{0,1:T(8,128)S(1)} collective-permute-done((f32[512,576]{0,1:T(8,128)S(1)}, f32[512,576]{0,1:T(8,128)S(1)}, u32[]{:S(2)}, u32[]{:S(2)}) %collective-permute-start.4) | collective-permute-done | bytes 1179680 | tf_op jit(solution)/shard_map/ppermute | solution.py:19
  173.9 1.8 add_add_fusion
  177.2 2.6 copy.66
  181.4 93.4 %all-reduce.1 = bf16[512,576]{0,1:T(8,128)(2,1)} all-reduce(f32[512,576]{0,1:T(8,128)S(1)} %pad_maximum_fusion.2), channel_id=1, replica_groups=mesh['ctx'=32,'head'=8] {'head'}, use_global_device_ids=true, to_apply=%region_7.9 | all-reduce | flops 294912 | bytes 1769472 | tf_op jit(solution)/shard_map/psum | solution.py:153
  274.8 51.4 %reduce-scatter.4.cloned.1.call-done = f32[16,512]{1,0:T(8,128)} async-done(((f32[512,512]{1,0:T(8,128)}), f32[16,512]{1,0:T(8,128)}) %reduce-scatter.4.cloned.1.call-update) | async-done | bytes 32784
  (160 shorter events, 53.2 us)
Async XLA Ops:
  7.2 27.5 %copy-start = (bf16[512,512]{1,0:T(8,128)(2,1)S(1)}, bf16[512,512]{1,0:T(8,128)(2,1)}, u32[]{:S(2)}) copy-start(bf16[512,512]{1,0:T(8,128)(2,1)} %param.14) | copy-start | bytes 1572868
  7.2 13.4 %copy-start.1 = (s32[16384]{0:T(1024)S(1)}, s32[16384]{0:T(1024)}, u32[]{:S(2)}) copy-start(s32[16384]{0:T(1024)} %param.15) | copy-start | bytes 196612
  7.2 319.0 %reduce-scatter.4.cloned.1.call-start = ((), (), s32[]{:S(2)}) async-start(), calls=%async_computation.1 | async-start | bytes 1081344
  7.2 13.5 %collective-permute-start = (bf16[512,576]{0,1:T(8,128)(2,1)}, bf16[512,576]{0,1:T(8,128)(2,1)}, u32[]{:S(2)}, u32[]{:S(2)}) collective-permute-start(bf16[512,576]{0,1:T(8,128)(2,1)} %param.11), channel_id=1, source_target_pairs={{0,24},{8,32},{16,40},{24,48},{32,56},{40,64},{48,72},{56,80},{64,... | collective-permute-start | bytes 1769480 | tf_op jit(solution)/shard_map/ppermute | solution.py:19
  11.0 22.2 %collective-permute-start.1 = (bf16[512,576]{0,1:T(8,128)(2,1)}, bf16[512,576]{0,1:T(8,128)(2,1)}, u32[]{:S(2)}, u32[]{:S(2)}) collective-permute-start(bf16[512,576]{0,1:T(8,128)(2,1)} %param.11), channel_id=1, source_target_pairs={{0,16},{8,24},{16,32},{24,40},{32,48},{40,56},{48,64},{56,72},{64,... | collective-permute-start | bytes 1769480 | tf_op jit(solution)/shard_map/ppermute | solution.py:19
  15.6 18.8 %collective-permute-start.2 = (bf16[512,576]{0,1:T(8,128)(2,1)}, bf16[512,576]{0,1:T(8,128)(2,1)S(1)}, u32[]{:S(2)}, u32[]{:S(2)}) collective-permute-start(bf16[512,576]{0,1:T(8,128)(2,1)} %param.11), channel_id=1, source_target_pairs={{0,8},{8,16},{16,24},{24,32},{32,40},{40,48},{48,56},{56,64},{64,7... | collective-permute-start | bytes 1769480 | tf_op jit(solution)/shard_map/ppermute | solution.py:19
  20.4 14.1 %copy-start.2 = (bf16[512,576]{0,1:T(8,128)(2,1)S(1)}, bf16[512,576]{0,1:T(8,128)(2,1)}, u32[]{:S(2)}) copy-start(bf16[512,576]{0,1:T(8,128)(2,1)} %param.11) | copy-start | bytes 1769476
  36.0 1.7 copy-start.4
  121.0 6.8 %collective-permute-start.3 = (f32[512,576]{0,1:T(8,128)S(1)}, f32[512,576]{0,1:T(8,128)S(1)}, u32[]{:S(2)}, u32[]{:S(2)}) collective-permute-start(f32[512,576]{0,1:T(8,128)S(1)} %get-tuple-element.637), channel_id=1, source_target_pairs={{8,0},{16,8},{24,16},{32,24},{40,32},{48,40},{56,48},{64,56},{72,6... | collective-permute-start | bytes 3538952 | tf_op jit(solution)/shard_map/ppermute | solution.py:19
  122.3 39.5 %collective-permute-start.5 = (f32[512,576]{0,1:T(8,128)S(1)}, f32[512,576]{0,1:T(8,128)S(1)}, u32[]{:S(2)}, u32[]{:S(2)}) collective-permute-start(f32[512,576]{0,1:T(8,128)S(1)} %get-tuple-element.638), channel_id=1, source_target_pairs={{24,0},{32,8},{40,16},{48,24},{56,32},{64,40},{72,48},{80,56},{88,... | collective-permute-start | bytes 3538952 | tf_op jit(solution)/shard_map/ppermute | solution.py:19
  123.6 52.1 %copy-start.3 = (bf16[512,576]{0,1:T(8,128)(2,1)S(1)}, bf16[512,576]{0,1:T(8,128)(2,1)}, u32[]{:S(2)}) copy-start(bf16[512,576]{0,1:T(8,128)(2,1)} %param.11) | copy-start | bytes 1769476
  123.6 50.3 %collective-permute-start.4 = (f32[512,576]{0,1:T(8,128)S(1)}, f32[512,576]{0,1:T(8,128)S(1)}, u32[]{:S(2)}, u32[]{:S(2)}) collective-permute-start(f32[512,576]{0,1:T(8,128)S(1)} %get-tuple-element.639), channel_id=1, source_target_pairs={{16,0},{24,8},{32,16},{40,24},{48,32},{56,40},{64,48},{72,56},{80,... | collective-permute-start | bytes 3538952 | tf_op jit(solution)/shard_map/ppermute | solution.py:19
Sparse Core Ops, SparseCore 0:
  179.9 146.2 reduce-scatter.3
where the time goes:
time: 334 us; the launch traced here: 333 us
  waiting for transfers between devices  112 us (34%)
  blocking collectives  93.4 us (28%)
  local copies, waits for them, and re-layouts  48.3 us (14%)
  matrix products  37.2 us (11%)
  between operations  14.3 us (4%)
  starting transfers between devices  14 us (4%)
  other arithmetic  13.3 us (4%)
    psum x1, blocking collectives, local(): lax.psum(jnp.concatenate([latent_part, rope_grad], axis=1), 'head')  93.4 us
    ppermute x6, waiting for transfers between devices, from_behind(): lax.ppermute(value, axis, [(source, source + steps) for source in range(i...  60.3 us
    unnamed x2, waiting for transfers between devices  51.4 us
    gather x8, local copies, waits for them, and re-layouts, block_parts(): key_docs = jnp.take(doc_ids, jnp.clip(key_pos, 0, token_total - 1))  25.1 us
    ppermute x6, starting transfers between devices, from_behind(): lax.ppermute(value, axis, [(source, source + steps) for source in range(i...  14 us
    dot_general x8, matrix products, block_parts(): jnp.einsum('thd,kd->htk', query_rope, key_rope, preferred_element_type=jn...  13.2 us
    unnamed x19, local copies, waits for them, and re-layouts  9.15 us
    slice x8, local copies, waits for them, and re-layouts, block_parts(): pairs = key_rows[:, :kv_width].reshape(KEY_BLOCK, head_count, NOPE + VDIM)  8.67 us
  transfers between devices with their start and end apart: 7, of which 5 were waited for; matrix products, arithmetic and copies ran while one was open for 2% of the time, Pallas kernels for 0%

commit v1 on v0

--- a/solution.py
+++ b/solution.py
@@ -150,7 +150,9 @@
     latent_part = lax.dot_general(
         kv_grad, kv_up_weight, (((1,), (1,)), ((), ())), preferred_element_type=jnp.float32
     )
-    latent_total = lax.psum(jnp.concatenate([latent_part, rope_grad], axis=1), "head")
+    latent_total = jnp.sum(
+        lax.all_gather(jnp.concatenate([latent_part, rope_grad], axis=1), "head"), axis=0
+    )
     latent_cols = lax.slice_in_dim(
         kv_latent, 0, lax.axis_size("ctx") * (LATENT // lax.axis_size("ctx")), axis=1
     )

time: 334 us -> 385 us (1.15)
  waiting for transfers between devices: 112 us -> 237 us
  blocking collectives: 93.4 us -> 0 us
  local copies, waits for them, and re-layouts: 48.3 us -> 59.9 us
  other arithmetic: 13.3 us -> 18.9 us
    all_gather x0 -> x1, waiting for transfers between devices: none -> 145 us  [local(): lax.all_gather(jnp.concatenate([latent_part, rope_grad], axis=1), 'head')]
    psum x1 -> x0, blocking collectives: 93.4 us -> none  [local(): lax.psum(jnp.concatenate([latent_part, rope_grad], axis=1), 'head')]
    unnamed x2 -> x3, waiting for transfers between devices: 51.4 us -> 31 us
    unnamed x19 -> x18, local copies, waits for them, and re-layouts: 9.15 us -> 20.8 us
    reduce_sum x0 -> x1, other arithmetic: none -> 4.56 us  [local(): jnp.sum(lax.all_gather(jnp.concatenate([latent_part, rope_grad], axis=1),...]
  transfers between devices with their start and end apart: 7 -> 8, of which waited for: 5 -> 6; matrix products, arithmetic and copies ran while one was open for 2% -> 7% of each run, Pallas kernels for 0% -> 0%
where the time goes in v1:
time: 385 us; the launch traced here: 383 us
  waiting for transfers between devices  237 us (62%)
  local copies, waits for them, and re-layouts  59.9 us (16%)
  matrix products  37.2 us (10%)
  other arithmetic  18.9 us (5%)
  between operations  15.8 us (4%)
  starting transfers between devices  14.1 us (4%)
    all_gather x1, waiting for transfers between devices, local(): lax.all_gather(jnp.concatenate([latent_part, rope_grad], axis=1), 'head')  145 us
    ppermute x6, waiting for transfers between devices, from_behind(): lax.ppermute(value, axis, [(source, source + steps) for source in range(i...  60.4 us
    unnamed x3, waiting for transfers between devices  31 us
    gather x8, local copies, waits for them, and re-layouts, block_parts(): key_docs = jnp.take(doc_ids, jnp.clip(key_pos, 0, token_total - 1))  25.1 us
    unnamed x18, local copies, waits for them, and re-layouts  20.8 us
    ppermute x6, starting transfers between devices, from_behind(): lax.ppermute(value, axis, [(source, source + steps) for source in range(i...  13.8 us
    dot_general x8, matrix products, block_parts(): jnp.einsum('thd,kd->htk', query_rope, key_rope, preferred_element_type=jn...  13.2 us
    slice x8, local copies, waits for them, and re-layouts, block_parts(): pairs = key_rows[:, :kv_width].reshape(KEY_BLOCK, head_count, NOPE + VDIM)  8.67 us
  transfers between devices with their start and end apart: 8, of which 6 were waited for; matrix products, arithmetic and copies ran while one was open for 7% of the time, Pallas kernels for 0%

profile of v1, /device:TPU:24, one launch (start us, length us, event | category | flops | bytes accessed | tf_op | source)
XLA Modules:
  0.0 383.3 jit_solution(459882192040848725)
XLA Ops:
  8.1 3.8 collective-permute-start
  11.9 4.6 %collective-permute-start.1 = (bf16[512,576]{0,1:T(8,128)(2,1)}, bf16[512,576]{0,1:T(8,128)(2,1)}, u32[]{:S(2)}, u32[]{:S(2)}) collective-permute-start(bf16[512,576]{0,1:T(8,128)(2,1)} %param.11), channel_id=1, source_target_pairs={{0,16},{8,24},{16,32},{24,40},{32,48},{40,56},{48,64},{56,72},{64,... | collective-permute-start | bytes 1769480 | tf_op jit(solution)/shard_map/ppermute | solution.py:19
  16.5 1.6 collective-permute-start.2
  22.7 11.4 %collective-permute-done.1 = bf16[512,576]{0,1:T(8,128)(2,1)} collective-permute-done((bf16[512,576]{0,1:T(8,128)(2,1)}, bf16[512,576]{0,1:T(8,128)(2,1)}, u32[]{:S(2)}, u32[]{:S(2)}) %collective-permute-start.1) | collective-permute-done | bytes 589856 | tf_op jit(solution)/shard_map/ppermute | solution.py:19
  36.8 1.7 pad_maximum_fusion.1
  38.5 32.1 %while.36 = (s32[]{:T(128)}, f32[2,512]{1,0:T(2,128)S(1)}, f32[2,512]{1,0:T(2,128)S(1)}, f32[2,512]{1,0:T(2,128)S(1)}, s32[512]{0:T(512)S(1)}, /*index=5*/s32[]{...) while((s32[]{:T(128)}, f32[2,512]{1,0:T(2,128)S(1)}, ...), condition=%wide.region_4.6_spmd.clone, body=%wide.region_0.5_spmd.clone.sunk | while | flops 342376960 | bytes 13933842 | solution.py:85
  38.6 3.1 gather_fusion
  46.6 3.1 gather_fusion
  51.7 1.6 fusion.95
  54.6 3.1 gather_fusion
  59.7 1.6 fusion.95
  62.6 3.1 gather_fusion
  67.7 1.6 fusion.95
  70.6 2.7 broadcast_in_dim.131
  73.3 46.1 %while.37 = (s32[]{:T(128)}, f32[512,2,128]{0,2,1:T(8,128)S(1)}, f32[512,2,64]{0,2,1:T(8,128)S(1)}, f32[2048,576]{0,1:T(8,128)}, bf16[2048,576]{0,1:T(8,128)(2,1...) while((s32[]{:T(128)}, f32[512,2,128]{0,2,1:T(8,128)S(1)}, ...), condition=%wide.region_6.8_spmd.clone, body=%wide.region_5.7_spmd.clone.sunk | while | flops 879502848 | bytes 26778924 | solution.py:131
  73.4 3.1 gather_fusion.1
  78.4 1.7 fusion.116
  84.9 3.1 gather_fusion.1
  89.9 1.7 fusion.116
  96.4 3.1 gather_fusion.1
  101.4 1.7 fusion.116
  107.9 3.1 gather_fusion.1
  113.0 1.7 fusion.116
  119.4 2.3 fusion.37
  125.7 2.9 collective-permute-done.3
  128.6 34.0 %collective-permute-done.5 = f32[512,576]{0,1:T(8,128)S(1)} collective-permute-done((f32[512,576]{0,1:T(8,128)S(1)}, f32[512,576]{0,1:T(8,128)S(1)}, u32[]{:S(2)}, u32[]{:S(2)}) %collective-permute-start.5) | collective-permute-done | bytes 1179680 | tf_op jit(solution)/shard_map/ppermute | solution.py:19
  162.6 12.1 %collective-permute-done.4 = f32[512,576]{0,1:T(8,128)S(1)} collective-permute-done((f32[512,576]{0,1:T(8,128)S(1)}, f32[512,576]{0,1:T(8,128)S(1)}, u32[]{:S(2)}, u32[]{:S(2)}) %collective-permute-start.4) | collective-permute-done | bytes 1179680 | tf_op jit(solution)/shard_map/ppermute | solution.py:19
  174.7 1.8 add_add_fusion
  182.2 145.3 %all-gather.3.cloned.1.call-done = f32[4096,576]{0,1:T(8,128)} async-done(((f32[512,576]{0,1:T(8,128)}), f32[4096,576]{0,1:T(8,128)}) %all-gather.3.cloned.1.call-update) | async-done | bytes 9437200 | tf_op jit(solution)/shard_map/all_gather | solution.py:154
  327.5 12.9 %copy.72 = f32[72,8,8,512]{3,2,1,0:T(8,128)S(1)} copy(f32[72,8,8,512]{3,1,2,0:T(8,128)} %bitcast.148) | data formatting | bytes 18874368
  340.4 4.6 %bitcast_reduce_fusion = bf16[512,576]{0,1:T(8,128)(2,1)} fusion(f32[72,8,8,512]{3,2,1,0:T(8,128)S(1)} %copy.72), kind=kLoop, calls=%fused_computation.65 | loop fusion | flops 2064384 | bytes 10027008 | tf_op jit(solution)/shard_map/reduce_sum | solution.py:153
  344.9 30.9 %reduce-scatter.4.cloned.1.call-done = f32[16,512]{1,0:T(8,128)} async-done(((f32[512,512]{1,0:T(8,128)}), f32[16,512]{1,0:T(8,128)}) %reduce-scatter.4.cloned.1.call-update) | async-done | bytes 32784
  (162 shorter events, 57.3 us)
Async XLA Ops:
  8.0 27.5 %copy-start = (bf16[512,512]{1,0:T(8,128)(2,1)S(1)}, bf16[512,512]{1,0:T(8,128)(2,1)}, u32[]{:S(2)}) copy-start(bf16[512,512]{1,0:T(8,128)(2,1)} %param.14) | copy-start | bytes 1572868
  8.0 13.4 %copy-start.1 = (s32[16384]{0:T(1024)S(1)}, s32[16384]{0:T(1024)}, u32[]{:S(2)}) copy-start(s32[16384]{0:T(1024)} %param.15) | copy-start | bytes 196612
  8.0 319.5 %all-gather.3.cloned.1.call-start = ((), (), s32[]{:S(2)}) async-start(), calls=%async_computation.1 | async-start | bytes 10616832 | tf_op jit(solution)/shard_map/all_gather | solution.py:154
  8.1 13.5 %collective-permute-start = (bf16[512,576]{0,1:T(8,128)(2,1)}, bf16[512,576]{0,1:T(8,128)(2,1)}, u32[]{:S(2)}, u32[]{:S(2)}) collective-permute-start(bf16[512,576]{0,1:T(8,128)(2,1)} %param.11), channel_id=1, source_target_pairs={{0,24},{8,32},{16,40},{24,48},{32,56},{40,64},{48,72},{56,80},{64,... | collective-permute-start | bytes 1769480 | tf_op jit(solution)/shard_map/ppermute | solution.py:19
  11.9 22.2 %collective-permute-start.1 = (bf16[512,576]{0,1:T(8,128)(2,1)}, bf16[512,576]{0,1:T(8,128)(2,1)}, u32[]{:S(2)}, u32[]{:S(2)}) collective-permute-start(bf16[512,576]{0,1:T(8,128)(2,1)} %param.11), channel_id=1, source_target_pairs={{0,16},{8,24},{16,32},{24,40},{32,48},{40,56},{48,64},{56,72},{64,... | collective-permute-start | bytes 1769480 | tf_op jit(solution)/shard_map/ppermute | solution.py:19
  16.5 18.8 %collective-permute-start.2 = (bf16[512,576]{0,1:T(8,128)(2,1)}, bf16[512,576]{0,1:T(8,128)(2,1)S(1)}, u32[]{:S(2)}, u32[]{:S(2)}) collective-permute-start(bf16[512,576]{0,1:T(8,128)(2,1)} %param.11), channel_id=1, source_target_pairs={{0,8},{8,16},{16,24},{24,32},{32,40},{40,48},{48,56},{56,64},{64,7... | collective-permute-start | bytes 1769480 | tf_op jit(solution)/shard_map/ppermute | solution.py:19
  21.3 14.1 %copy-start.2 = (bf16[512,576]{0,1:T(8,128)(2,1)S(1)}, bf16[512,576]{0,1:T(8,128)(2,1)}, u32[]{:S(2)}) copy-start(bf16[512,576]{0,1:T(8,128)(2,1)} %param.11) | copy-start | bytes 1769476
  36.8 1.7 copy-start.3
  121.8 6.8 %collective-permute-start.3 = (f32[512,576]{0,1:T(8,128)S(1)}, f32[512,576]{0,1:T(8,128)S(1)}, u32[]{:S(2)}, u32[]{:S(2)}) collective-permute-start(f32[512,576]{0,1:T(8,128)S(1)} %get-tuple-element.637), channel_id=1, source_target_pairs={{8,0},{16,8},{24,16},{32,24},{40,32},{48,40},{56,48},{64,56},{72,6... | collective-permute-start | bytes 3538952 | tf_op jit(solution)/shard_map/ppermute | solution.py:19
  123.1 39.5 %collective-permute-start.5 = (f32[512,576]{0,1:T(8,128)S(1)}, f32[512,576]{0,1:T(8,128)S(1)}, u32[]{:S(2)}, u32[]{:S(2)}) collective-permute-start(f32[512,576]{0,1:T(8,128)S(1)} %get-tuple-element.638), channel_id=1, source_target_pairs={{24,0},{32,8},{40,16},{48,24},{56,32},{64,40},{72,48},{80,56},{88,... | collective-permute-start | bytes 3538952 | tf_op jit(solution)/shard_map/ppermute | solution.py:19
  124.4 50.3 %collective-permute-start.4 = (f32[512,576]{0,1:T(8,128)S(1)}, f32[512,576]{0,1:T(8,128)S(1)}, u32[]{:S(2)}, u32[]{:S(2)}) collective-permute-start(f32[512,576]{0,1:T(8,128)S(1)} %get-tuple-element.639), channel_id=1, source_target_pairs={{16,0},{24,8},{32,16},{40,24},{48,32},{56,40},{64,48},{72,56},{80,... | collective-permute-start | bytes 3538952 | tf_op jit(solution)/shard_map/ppermute | solution.py:19
  178.1 197.8 %reduce-scatter.4.cloned.1.call-start = ((), (), s32[]{:S(2)}) async-start(), calls=%async_computation.2 | async-start | bytes 1081344
Sparse Core Ops, SparseCore 0:
  178.2 149.2 all-gather.2
Sparse Core Ops, SparseCore 1:
  181.6 194.2 reduce-scatter.3
